TPU v7x, 512 devices: a whole 4x4x16 slice. The times are simulated.
512 devices in a mesh: rep: 16 (over x, z_lo), fsdp: 32 (over y, z_hi, core).
Axes of the slice: x: 4, y: 4, z: 16 (z_hi: 4, z_lo: 4; z = z_hi * 4 + z_lo), core: 2. Of those that a mesh axis runs over, the one named last changes fastest.
Arguments:
- inner_weights: bfloat16 [16, 512, 10240], P('rep', 'fsdp'), may hold values from -1000 to 1000
- master: float32 [512, 10240], P('fsdp'), may hold values from -6 to 6.5
- momentum: float32 [512, 10240], P('fsdp'), may hold values from -6 to 6
Outputs:
- new_master: float32 [512, 10240], P('fsdp')
- new_momentum: float32 [512, 10240], P('fsdp')
- working: bfloat16 [512, 10240], P('fsdp')
All inputs are finite; a program needn't handle non-finite values.
Results may differ from a plain program's by a relative error of at most 0.0015.
Values may be sent and summed in bfloat16 or wider, within the bound.
No kernel may reach another device: no remote copies, remote signals or barrier semaphores. Data moves between devices by JAX's collectives and lax.ppermute only.
A program may use at most 64 MiB of HBM per device.

v0:
```python
import math

import jax
import jax.numpy as jnp
from jax import lax
from jax.sharding import PartitionSpec as P


def outer_step(pseudo, master, momentum, squares, element_count):
    factor = jnp.minimum(1.0, 0.5 * math.sqrt(element_count) / jnp.sqrt(squares + 1e-06))
    clipped = factor * pseudo
    new_momentum = 0.9 * momentum + clipped
    new_master = master - 0.7 * (clipped + 0.9 * new_momentum)
    return (new_master, new_momentum)


def shards(inner_weights, master, momentum):
    replica_count = lax.axis_size("rep")
    element_count = master.shape[0] * lax.axis_size("fsdp") * master.shape[1]
    summed = lax.psum(master - inner_weights[0].astype(jnp.float32), "rep")
    pseudo = summed / replica_count
    squares = lax.psum(jnp.sum(pseudo * pseudo), "fsdp")
    new_master, new_momentum = outer_step(pseudo, master, momentum, squares, element_count)
    return (new_master, new_momentum, new_master.astype(jnp.bfloat16))


def solution(mesh):
    placed = (P("rep", "fsdp", None), P("fsdp", None), P("fsdp", None))
    return jax.shard_map(
        shards,
        mesh=mesh,
        in_specs=placed,
        out_specs=(P("fsdp", None), P("fsdp", None), P("fsdp", None)),
        check_vma=False,
    )
```

profile of v0, /device:TPU:1, one launch (start us, length us, event | category | flops | bytes accessed | tf_op | source)
XLA Modules:
  0.0 285.7 jit_solution(9544126834237275803)
XLA Ops:
  7.2 0.0 all-reduce.2.cloned.1.call-start
  7.2 0.0 copy-start.2
  7.2 2.1 convert_subtract_fusion
  9.3 0.0 copy-start
  9.4 0.0 all-reduce.2.cloned.1.call-update
  9.4 170.2 %all-reduce.2.cloned.1.call-done = f32[16,10240]{1,0:T(8,128)} async-done(((f32[16,10240]{1,0:T(8,128)}), f32[16,10240]{1,0:T(8,128)}) %all-reduce.2.cloned.1.call-update) | async-done | bytes 655376 | tf_op jit(solution)/shard_map/psum | solution.py:20
  179.6 0.0 copy-start.1
  179.6 1.9 multiply_reduce_fusion
  181.5 95.3 %psum.15 = f32[]{:T(128)} all-reduce(f32[]{:T(128)} %multiply_reduce_fusion), channel_id=1, replica_groups=mesh['rep'=16,'fsdp'=32] {'fsdp'}, use_global_device_ids=true, to_apply=%region_2.0 | all-reduce | flops 1 | bytes 8 | tf_op jit(solution)/shard_map/psum | solution.py:22
  277.5 0.0 copy-done.2
  277.5 0.0 copy-done
  277.5 0.0 copy-done.1
  277.5 1.3 fusion
Async XLA Ops:
  7.2 172.4 %all-reduce.2.cloned.1.call-start = ((), (), s32[]{:S(2)}) async-start(), calls=%async_computation | async-start | bytes 1310720 | tf_op jit(solution)/shard_map/psum | solution.py:20
  7.2 270.3 %copy-start.2 = (f32[16,10240]{1,0:T(8,128)S(1)}, f32[16,10240]{1,0:T(8,128)}, u32[]{:S(2)}) copy-start(f32[16,10240]{1,0:T(8,128)} %param.5) | copy-start | bytes 1966084
  9.3 268.1 %copy-start = (f32[16,10240]{1,0:T(8,128)S(1)}, f32[16,10240]{1,0:T(8,128)}, u32[]{:S(2)}) copy-start(f32[16,10240]{1,0:T(8,128)} %param.4) | copy-start | bytes 1966084
  179.6 97.9 %copy-start.1 = (f32[16,10240]{1,0:T(8,128)S(1)}, f32[16,10240]{1,0:T(8,128)}, u32[]{:S(2)}) copy-start(f32[16,10240]{1,0:T(8,128)} %all-reduce.2.cloned.1.call-done) | copy-start | bytes 1966084
Sparse Core Ops, SparseCore 0:
  11.5 168.0 all-reduce.1
where the time goes:
time: 286 us
  waiting for transfers between devices  170 us (59%)
  blocking collectives  95.3 us (33%)
  between operations  14.8 us (5%)
  other arithmetic  5.38 us (2%)
    psum x1, waiting for transfers between devices, shards(): summed = lax.psum(master - inner_weights[0].astype(jnp.float32), 'rep')  170 us
    psum x1, blocking collectives, shards(): squares = lax.psum(jnp.sum(pseudo * pseudo), 'fsdp')  95.3 us
  transfers between devices with their start and end apart: 1, of which 1 were waited for; matrix products, arithmetic and copies ran while one was open for 0% of the time, Pallas kernels for 0%

commit v1 on v0

--- a/solution.py
+++ b/solution.py
@@ -14,12 +14,27 @@
     return (new_master, new_momentum)
 
 
+def to_all(piece, axis):
+    copies = jnp.broadcast_to(piece[None], (lax.axis_size(axis),) + piece.shape)
+    return lax.all_to_all(copies, axis, 0, 0, tiled=True)
+
+
 def shards(inner_weights, master, momentum):
-    replica_count = lax.axis_size("rep")
-    element_count = master.shape[0] * lax.axis_size("fsdp") * master.shape[1]
-    summed = lax.psum(master - inner_weights[0].astype(jnp.float32), "rep")
-    pseudo = summed / replica_count
-    squares = lax.psum(jnp.sum(pseudo * pseudo), "fsdp")
+    replicas = lax.axis_size("rep")
+    rows, cols = master.shape
+    element_count = rows * lax.axis_size("fsdp") * cols
+    bands = rows // 8
+    across = replicas // bands
+    width = cols // across
+    pieces = inner_weights[0].reshape(bands, 8, across, width).transpose(0, 2, 1, 3).reshape(replicas, 8, width)
+    received = lax.all_to_all(pieces, "rep", 0, 0, tiled=True)
+    me = lax.axis_index("rep")
+    own = lax.dynamic_slice(master, (me // across * 8, me % across * width), (8, width))
+    summed = jnp.sum(own[None] - received.astype(jnp.float32), axis=0)
+    gathered = to_all(summed / replicas, "rep")
+    pseudo = gathered.reshape(bands, across, 8, width).transpose(0, 2, 1, 3).reshape(rows, cols)
+    shares = to_all(jnp.full((128,), jnp.sum(pseudo * pseudo)), "fsdp")
+    squares = jnp.sum(shares[:, 0])
     new_master, new_momentum = outer_step(pseudo, master, momentum, squares, element_count)
     return (new_master, new_momentum, new_master.astype(jnp.bfloat16))
 

time: 286 us -> 79.6 us (0.28)
  waiting for transfers between devices: 170 us -> 11.2 us
  blocking collectives: 95.3 us -> 52.8 us
  between operations: 14.8 us -> 1.42 us
  starting transfers between devices: 0.04 us -> 9.03 us
    psum x1 -> x0, waiting for transfers between devices: 170 us -> none  [shards(): summed = lax.psum(master - inner_weights[0].astype(jnp.float32), 'rep')]
    psum x1 -> x0, blocking collectives: 95.3 us -> none  [shards(): squares = lax.psum(jnp.sum(pseudo * pseudo), 'fsdp')]
    all_to_all x0 -> x2, blocking collectives: none -> 52.8 us  [to_all(): return lax.all_to_all(copies, axis, 0, 0, tiled=True)]
    all_to_all x0 -> x1, waiting for transfers between devices: none -> 11.2 us  [shards(): received = lax.all_to_all(pieces, 'rep', 0, 0, tiled=True)]
    all_to_all x0 -> x1, starting transfers between devices: none -> 9.03 us  [shards(): received = lax.all_to_all(pieces, 'rep', 0, 0, tiled=True)]
where the time goes in v1:
time: 79.6 us; the launch traced here: 79.3 us
  blocking collectives  52.8 us (66%)
  waiting for transfers between devices  11.2 us (14%)
  starting transfers between devices  9.03 us (11%)
  other arithmetic  2.81 us (4%)
  local copies, waits for them, and re-layouts  1.93 us (2%)
  between operations  1.42 us (2%)
    all_to_all x2, blocking collectives, to_all(): return lax.all_to_all(copies, axis, 0, 0, tiled=True)  52.8 us
    all_to_all x1, waiting for transfers between devices, shards(): received = lax.all_to_all(pieces, 'rep', 0, 0, tiled=True)  11.2 us
    all_to_all x1, starting transfers between devices, shards(): received = lax.all_to_all(pieces, 'rep', 0, 0, tiled=True)  9.03 us
  transfers between devices with their start and end apart: 1, of which 1 were waited for; matrix products, arithmetic and copies ran while one was open for 0% of the time, Pallas kernels for 0%

profile of v1, /device:TPU:1, one launch (start us, length us, event | category | flops | bytes accessed | tf_op | source)
XLA Modules:
  0.0 79.3 jit_solution(821387444131455016)
XLA Ops:
  0.6 9.0 %all-to-all-start = ((bf16[16,8,1280]{2,1,0:T(8,128)(2,1)}), bf16[16,8,1280]{2,1,0:T(8,128)(2,1)S(1)}, u32[]{:S(2)}, u32[]{:S(2)}) async-start(bf16[16,8,1280]{2,1,0:T(8,128)(2,1)} %bitcast.12), calls=%async_computation | async-start | bytes 655360 | tf_op jit(solution)/shard_map/all_to_all | solution.py:30
  9.7 0.0 dynamic-slice-start
  9.7 11.2 %all-to-all-done = bf16[16,8,1280]{2,1,0:T(8,128)(2,1)S(1)} async-done(((bf16[16,8,1280]{2,1,0:T(8,128)(2,1)}), bf16[16,8,1280]{2,1,0:T(8,128)(2,1)S(1)}, u32[]{:S(2)}, u32[]{:S(2)}) %all-to-all-start) | async-done | bytes 327712 | tf_op jit(solution)/shard_map/all_to_all | solution.py:30
  20.9 0.0 dynamic-slice-done
  20.9 0.1 subtract_reduce_fusion
  21.1 21.9 %all_to_all.19 = f32[16,8,1280]{2,1,0:T(8,128)S(1)} all-to-all(f32[16,8,1280]{2,1,0:T(8,128)S(1)} %broadcast_in_dim.2), channel_id=1, replica_groups=mesh['rep'=16,'fsdp'=32] {'rep'}, dimensions={0} | all-to-all | bytes 1310720 | tf_op jit(solution)/shard_map/all_to_all | solution.py:19
  43.0 0.8 multiply_reduce_fusion
  43.7 0.7 broadcast_in_dim_broadcast_in_dim_broadcast_in_dim.3
  44.4 31.0 %all_to_all.20 = f32[32,1,128]{2,1,0:T(1,128)S(1)} all-to-all(f32[32,1,128]{2,1,0:T(1,128)S(1)} %broadcast_in_dim_broadcast_in_dim_broadcast_in_dim.3), channel_id=1, replica_groups=mesh['rep'=16,'fsdp'=32] {'fsdp'}, dimensions={0} | all-to-all | bytes 32768 | tf_op jit(solution)/shard_map/all_to_all | solution.py:19
  75.4 0.6 slice_reduce_fusion
  76.6 0.0 copy-start
  76.7 0.0 copy-start.1
  76.7 1.0 %copy-done = f32[16,10240]{1,0:T(8,128)S(1)} copy-done((f32[16,10240]{1,0:T(8,128)S(1)}, f32[16,10240]{1,0:T(8,128)}, u32[]{:S(2)}) %copy-start) | copy-done | bytes 655384
  77.7 0.2 copy-done.1
  77.9 1.3 %fusion = (bf16[16,10240]{1,0:T(8,128)(2,1)}, f32[16,10240]{1,0:T(8,128)}, f32[16,10240]{1,0:T(8,128)}) fusion(f32[16,10240]{1,0:T(8,128)S(1)} %copy-done, f32[16,10240]{1,0:T(8,128)S(1)} %bitcast.11, f32[16,10240]{1,0:T(8,128)S(1)} %copy-done.1), kind=kLoop, calls=%fused_computation.7 | loop fusion | flops 1146880 | bytes 3604480 | tf_op jit(solution)/shard_map/convert_element_type | solution.py:39
  (3 shorter events, 0.1 us)
Async XLA Ops:
  0.6 20.3 %all-to-all-start = ((bf16[16,8,1280]{2,1,0:T(8,128)(2,1)}), bf16[16,8,1280]{2,1,0:T(8,128)(2,1)S(1)}, u32[]{:S(2)}, u32[]{:S(2)}) async-start(bf16[16,8,1280]{2,1,0:T(8,128)(2,1)} %bitcast.12), calls=%async_computation | async-start | bytes 655360 | tf_op jit(solution)/shard_map/all_to_all | solution.py:30
  9.7 11.2 %dynamic-slice-start = ((f32[16,10240]{1,0:T(8,128)}, s32[]{:T(128)}, s32[]{:T(128)}), f32[8,1280]{1,0:T(8,128)S(1)}, s32[]{:S(2)}) async-start(f32[16,10240]{1,0:T(8,128)} %param.4, s32[]{:T(128)} %select_n.18, s32[]{:T(128)} %select_n.20), calls=%async_computation.3 | async-start | bytes 82432 | tf_op jit(solution)/shard_map/dynamic_slice | solution.py:32
  76.6 1.1 %copy-start = (f32[16,10240]{1,0:T(8,128)S(1)}, f32[16,10240]{1,0:T(8,128)}, u32[]{:S(2)}) copy-start(f32[16,10240]{1,0:T(8,128)} %param.4) | copy-start | bytes 1966084
  76.7 1.3 %copy-start.1 = (f32[16,10240]{1,0:T(8,128)S(1)}, f32[16,10240]{1,0:T(8,128)}, u32[]{:S(2)}) copy-start(f32[16,10240]{1,0:T(8,128)} %param.5) | copy-start | bytes 1966084

commit v2 on v1

v2 whole, which is shorter than its diff:
```python
import math

import jax
import jax.numpy as jnp
from jax import lax
from jax.sharding import Mesh, PartitionSpec as P

SIZES = (4, 4, 4, 4, 2)
NAMES = ("x", "z_lo", "y", "z_hi", "core")
REP = ("x", "z_lo")
FSDP = ("y", "z_hi", "core")


def outer_step(pseudo, master, momentum, squares, element_count):
    factor = jnp.minimum(1.0, 0.5 * math.sqrt(element_count) / jnp.sqrt(squares + 1e-06))
    clipped = factor * pseudo
    new_momentum = 0.9 * momentum + clipped
    new_master = master - 0.7 * (clipped + 0.9 * new_momentum)
    return (new_master, new_momentum)


def position(x, z_lo, y, z_hi, core):
    place = 0
    for size, index in zip(SIZES, (x, z_lo, y, z_hi, core)):
        place = place * size + index
    return place


def near_groups():
    n_x, n_lo, n_y, n_hi, n_core = SIZES
    return [
        [
            position(x, (z_lo + n_lo // 2 * (z_hi * 2 // n_hi)) % n_lo, y, z_hi, core)
            for x in range(n_x)
            for y in range(n_y)
            for z_hi in range(n_hi)
            for core in range(n_core)
        ]
        for z_lo in range(n_lo)
    ]


def to_all(piece, size, axis, groups=None):
    copies = jnp.broadcast_to(piece[None], (size,) + piece.shape)
    return lax.all_to_all(copies, axis, 0, 0, axis_index_groups=groups, tiled=True)


def shards(inner_weights, master, momentum):
    replicas = lax.axis_size(REP)
    rows, cols = master.shape
    element_count = rows * lax.axis_size(FSDP) * cols
    bands = rows // 8
    across = replicas // bands
    width = cols // across
    pieces = inner_weights[0].reshape(bands, 8, across, width).transpose(0, 2, 1, 3).reshape(replicas, 8, width)
    received = lax.all_to_all(pieces, REP, 0, 0, tiled=True)
    me = lax.axis_index(REP)
    own = lax.dynamic_slice(master, (me // across * 8, me % across * width), (8, width))
    mean = jnp.sum(own[None] - received.astype(jnp.float32), axis=0) / replicas
    column = to_all(mean, lax.axis_size("z_lo"), "z_lo")
    groups = near_groups()
    shares = to_all(jnp.full((1, 128), jnp.sum(column * column)), len(groups[0]), NAMES, groups)
    gathered = lax.all_gather(column, "x")
    squares = jnp.sum(shares[:, 0, 0])
    pseudo = gathered.reshape(bands, across, 8, width).transpose(0, 2, 1, 3).reshape(rows, cols)
    new_master, new_momentum = outer_step(pseudo, master, momentum, squares, element_count)
    return (new_master, new_momentum, new_master.astype(jnp.bfloat16))


def solution(mesh):
    fine = Mesh(mesh.devices.reshape(SIZES), NAMES)
    rows = P(FSDP, None)
    return jax.shard_map(
        shards,
        mesh=fine,
        in_specs=(P(REP, FSDP, None), rows, rows),
        out_specs=(rows, rows, rows),
        check_vma=False,
    )
```

time: 79.6 us -> 68.3 us (0.86)
  blocking collectives: 52.8 us -> 20.6 us
  starting transfers between devices: 9.03 us -> 27.3 us
  waiting for transfers between devices: 11.2 us -> 13.4 us
    all_to_all x2 -> x1, blocking collectives: 52.8 us -> 7.93 us  [to_all(): lax.all_to_all(copies, axis, 0, 0, axis_index_groups=groups, tiled=True)]
    all_to_all x1 -> x2, starting transfers between devices: 9.03 us -> 27.3 us  [the longest x1 18.2 us: to_all(): lax.all_to_all(copies, axis, 0, 0, axis_index_groups=groups, tiled=True)]
    all_gather x0 -> x1, blocking collectives: none -> 12.6 us  [shards(): gathered = lax.all_gather(column, 'x')]
    all_to_all x1 -> x2, waiting for transfers between devices: 11.2 us -> 13.4 us  [the longest x1 11.2 us: shards(): received = lax.all_to_all(pieces, REP, 0, 0, tiled=True)]
  transfers between devices with their start and end apart: 1 -> 2, of which waited for: 1 -> 2; matrix products, arithmetic and copies ran while one was open for 0% -> 0% of each run, Pallas kernels for 0% -> 0%
where the time goes in v2:
time: 68.3 us; the launch traced here: 68 us
  starting transfers between devices  27.3 us (40%)
  blocking collectives  20.6 us (30%)
  waiting for transfers between devices  13.4 us (20%)
  other arithmetic  2.81 us (4%)
  local copies, waits for them, and re-layouts  2.55 us (4%)
  between operations  1.42 us (2%)
    all_to_all x1, starting transfers between devices, to_all(): lax.all_to_all(copies, axis, 0, 0, axis_index_groups=groups, tiled=True)  18.2 us
    all_gather x1, blocking collectives, shards(): gathered = lax.all_gather(column, 'x')  12.6 us
    all_to_all x1, waiting for transfers between devices, shards(): received = lax.all_to_all(pieces, REP, 0, 0, tiled=True)  11.2 us
    all_to_all x1, starting transfers between devices, shards(): received = lax.all_to_all(pieces, REP, 0, 0, tiled=True)  9.03 us
    all_to_all x1, blocking collectives, to_all(): lax.all_to_all(copies, axis, 0, 0, axis_index_groups=groups, tiled=True)  7.93 us
    all_to_all x1, waiting for transfers between devices, to_all(): lax.all_to_all(copies, axis, 0, 0, axis_index_groups=groups, tiled=True)  2.17 us
  transfers between devices with their start and end apart: 2, of which 2 were waited for; matrix products, arithmetic and copies ran while one was open for 0% of the time, Pallas kernels for 0%

profile of v2, /device:TPU:1, one launch (start us, length us, event | category | flops | bytes accessed | tf_op | source)
XLA Modules:
  0.0 68.0 jit_solution(10646677039892348098)
XLA Ops:
  0.6 9.0 %all-to-all-start = ((bf16[16,8,1280]{2,1,0:T(8,128)(2,1)}), bf16[16,8,1280]{2,1,0:T(8,128)(2,1)S(1)}, u32[]{:S(2)}, u32[]{:S(2)}) async-start(bf16[16,8,1280]{2,1,0:T(8,128)(2,1)} %bitcast.11), calls=%async_computation | async-start | bytes 655360 | tf_op jit(solution)/shard_map/all_to_all | solution.py:56
  9.7 0.0 dynamic-slice-start
  9.7 11.2 %all-to-all-done = bf16[16,8,1280]{2,1,0:T(8,128)(2,1)S(1)} async-done(((bf16[16,8,1280]{2,1,0:T(8,128)(2,1)}), bf16[16,8,1280]{2,1,0:T(8,128)(2,1)S(1)}, u32[]{:S(2)}, u32[]{:S(2)}) %all-to-all-start) | async-done | bytes 327712 | tf_op jit(solution)/shard_map/all_to_all | solution.py:56
  20.9 0.0 dynamic-slice-done
  20.9 0.1 subtract_reduce_fusion
  21.0 7.9 %all_to_all.15 = f32[4,8,1280]{2,1,0:T(8,128)S(1)} all-to-all(f32[4,8,1280]{2,1,0:T(8,128)S(1)} %broadcast_in_dim.2), channel_id=1, replica_groups=mesh['x'=4,'z_lo'=4,'y'=4,'z_hi'=4,'core'=2] {'z_lo'}, dimensions={0} | all-to-all | bytes 327680 | tf_op jit(solution)/shard_map/all_to_all | solution.py:45
  29.0 0.6 multiply_reduce_fusion
  29.6 1.3 %broadcast_in_dim_broadcast_in_dim_broadcast_in_dim.3 = f32[128,1,128]{2,1,0:T(1,128)} broadcast(f32[]{:T(128)} %multiply_reduce_fusion), dimensions={} | broadcast | bytes 65540 | tf_op jit(solution)/shard_map/broadcast_in_dim;broadcast_in_dim;broadcast_in_dim | solution.py:44
  30.9 18.2 %all-to-all-start.2 = ((f32[128,1,128]{2,1,0:T(1,128)}), f32[128,1,128]{2,1,0:T(1,128)S(1)}, u32[]{:S(2)}, u32[]{:S(2)}) async-start(f32[128,1,128]{2,1,0:T(1,128)} %broadcast_in_dim_broadcast_in_dim_broadcast_in_dim.3), calls=%async_computation.2 | async-start | bytes 131072 | tf_op jit(solution)/shard_map/all_to_all | solution.py:45
  49.2 12.6 %all-gather = f32[16,8,1280]{2,1,0:T(8,128)S(1)} all-gather(f32[4,8,1280]{2,1,0:T(8,128)S(1)} %all_to_all.15), channel_id=2, replica_groups=mesh['x'=4,'z_lo'=4,'y'=4,'z_hi'=4,'core'=2] {'x'}, dimensions={0}, use_global_device_ids=true | all-gather | bytes 819200 | tf_op jit(solution)/shard_map/all_gather | solution.py:63
  61.8 2.2 %all-to-all-done.2 = f32[128,1,128]{2,1,0:T(1,128)S(1)} async-done(((f32[128,1,128]{2,1,0:T(1,128)}), f32[128,1,128]{2,1,0:T(1,128)S(1)}, u32[]{:S(2)}, u32[]{:S(2)}) %all-to-all-start.2) | async-done | bytes 65568 | tf_op jit(solution)/shard_map/all_to_all | solution.py:45
  64.0 0.7 %slice_reduce_fusion = f32[]{:T(128)} fusion(f32[128,1,128]{2,1,0:T(1,128)S(1)} %all-to-all-done.2), kind=kLoop, calls=%fused_computation.5 | loop fusion | flops 127 | bytes 516 | tf_op jit(solution)/shard_map/reduce_sum | solution.py:64
  65.4 0.0 copy-start
  65.4 0.0 copy-start.1
  65.5 1.0 %copy-done = f32[16,10240]{1,0:T(8,128)S(1)} copy-done((f32[16,10240]{1,0:T(8,128)S(1)}, f32[16,10240]{1,0:T(8,128)}, u32[]{:S(2)}) %copy-start) | copy-done | bytes 655384
  66.5 0.2 copy-done.1
  66.7 1.3 %fusion = (bf16[16,10240]{1,0:T(8,128)(2,1)}, f32[16,10240]{1,0:T(8,128)}, f32[16,10240]{1,0:T(8,128)}) fusion(f32[16,10240]{1,0:T(8,128)S(1)} %copy-done, f32[16,10240]{1,0:T(8,128)S(1)} %bitcast.10, f32[16,10240]{1,0:T(8,128)S(1)} %copy-done.1), kind=kLoop, calls=%fused_computation.7 | loop fusion | flops 1146880 | bytes 3604480 | tf_op jit(solution)/shard_map/convert_element_type | solution.py:67
  (3 shorter events, 0.1 us)
Async XLA Ops:
  0.6 20.3 %all-to-all-start = ((bf16[16,8,1280]{2,1,0:T(8,128)(2,1)}), bf16[16,8,1280]{2,1,0:T(8,128)(2,1)S(1)}, u32[]{:S(2)}, u32[]{:S(2)}) async-start(bf16[16,8,1280]{2,1,0:T(8,128)(2,1)} %bitcast.11), calls=%async_computation | async-start | bytes 655360 | tf_op jit(solution)/shard_map/all_to_all | solution.py:56
  9.7 11.2 %dynamic-slice-start = ((f32[16,10240]{1,0:T(8,128)}, s32[]{:T(128)}, s32[]{:T(128)}), f32[8,1280]{1,0:T(8,128)S(1)}, s32[]{:S(2)}) async-start(f32[16,10240]{1,0:T(8,128)} %param.4, s32[]{:T(128)} %select_n.18, s32[]{:T(128)} %select_n.20), calls=%async_computation.3 | async-start | bytes 82432 | tf_op jit(solution)/shard_map/dynamic_slice | solution.py:58
  30.9 33.0 %all-to-all-start.2 = ((f32[128,1,128]{2,1,0:T(1,128)}), f32[128,1,128]{2,1,0:T(1,128)S(1)}, u32[]{:S(2)}, u32[]{:S(2)}) async-start(f32[128,1,128]{2,1,0:T(1,128)} %broadcast_in_dim_broadcast_in_dim_broadcast_in_dim.3), calls=%async_computation.2 | async-start | bytes 131072 | tf_op jit(solution)/shard_map/all_to_all | solution.py:45
  65.4 1.1 %copy-start = (f32[16,10240]{1,0:T(8,128)S(1)}, f32[16,10240]{1,0:T(8,128)}, u32[]{:S(2)}) copy-start(f32[16,10240]{1,0:T(8,128)} %param.4) | copy-start | bytes 1966084
  65.4 1.3 %copy-start.1 = (f32[16,10240]{1,0:T(8,128)S(1)}, f32[16,10240]{1,0:T(8,128)}, u32[]{:S(2)}) copy-start(f32[16,10240]{1,0:T(8,128)} %param.5) | copy-start | bytes 1966084

commit v3 on v2

v3 whole, which is shorter than its diff:
```python
import math

import jax
import jax.numpy as jnp
from jax import lax
from jax.experimental import pallas as pl
from jax.experimental.pallas import tpu as pltpu
from jax.sharding import Mesh, PartitionSpec as P

SIZES = (4, 4, 4, 4, 2)
NAMES = ("x", "z_lo", "y", "z_hi", "core")
REP = ("x", "z_lo")
FSDP = ("y", "z_hi", "core")
LANES = 128
SUBLANES = 8
OUT_CHUNKS = 4
PIECE_START = (2, 2)
SHARE_START = (0, 0, 3)


def turned(size, start):
    return [(start + step) % size for step in range(size)]


def position(x, z_lo, y, z_hi, core):
    place = 0
    for size, index in zip(SIZES, (x, z_lo, y, z_hi, core)):
        place = place * size + index
    return place


def near_groups():
    n_x, n_lo, n_y, n_hi, n_core = SIZES
    from_x, from_y, from_hi = SHARE_START
    return [
        [
            position(x, (z_lo + n_lo // 2 * (z_hi * 2 // n_hi)) % n_lo, y, z_hi, core)
            for x in turned(n_x, from_x)
            for y in turned(n_y, from_y)
            for z_hi in turned(n_hi, from_hi)
            for core in range(n_core)
        ]
        for z_lo in range(n_lo)
    ]


def squares_kernel(column_ref, shares_ref):
    pieces, _, width = column_ref.shape
    total = jnp.zeros((SUBLANES, LANES), jnp.float32)
    for piece in range(pieces):
        for start in range(0, width, LANES):
            value = column_ref[piece, :, start : start + LANES]
            total = total + value * value
    lanes = jnp.sum(total, axis=0, keepdims=True)
    shares_ref[...] = jnp.broadcast_to(lanes, shares_ref.shape)


def finish_kernel(
    element_count, shares_ref, pseudo_ref, master_ref, momentum_ref,
    new_master_ref, new_momentum_ref, working_ref,
    master_slot, momentum_slot, working_slot, sems,
):
    pieces, _, width = pseudo_ref.shape
    rows, cols = master_ref.shape
    bands = rows // SUBLANES
    across = pieces // bands
    squares = jnp.sum(shares_ref[...], keepdims=True)
    factor = jnp.minimum(1.0, 0.5 * math.sqrt(element_count) * lax.rsqrt(squares + 1e-06))
    copies = []
    chunk = cols // OUT_CHUNKS
    for block in range(across):
        at = slice(block * width, (block + 1) * width)
        pseudo = jnp.concatenate([pseudo_ref[band * across + block] for band in range(bands)], axis=0)
        clipped = factor * pseudo
        new_momentum = 0.9 * momentum_ref[:, at] + clipped
        new_master = master_ref[:, at] - 0.7 * (clipped + 0.9 * new_momentum)
        momentum_slot[:, at] = new_momentum
        master_slot[:, at] = new_master
        working_slot[:, at] = new_master.astype(jnp.bfloat16)
        done = (block + 1) * width
        if done % chunk == 0:
            part = slice(done - chunk, done)
            pairs = ((master_slot, new_master_ref), (momentum_slot, new_momentum_ref), (working_slot, working_ref))
            for k, (slot, out) in enumerate(pairs):
                copy = pltpu.make_async_copy(slot.at[:, part], out.at[:, part], sems.at[k, done // chunk - 1])
                copy.start()
                copies.append(copy)
    for copy in copies:
        copy.wait()


def shards(inner_weights, master, momentum):
    replicas = lax.axis_size(REP)
    rows, cols = master.shape
    element_count = rows * lax.axis_size(FSDP) * cols
    bands = rows // SUBLANES
    across = replicas // bands
    width = cols // across
    pieces = inner_weights[0].reshape(bands, SUBLANES, across, width).transpose(0, 2, 1, 3).reshape(replicas, SUBLANES, width)
    n_x, n_lo = lax.axis_size("x"), lax.axis_size("z_lo")
    from_x, from_lo = PIECE_START
    along_x, along_lo = turned(n_x, from_x), turned(n_lo, from_lo)
    along_rep = [x * n_lo + z_lo for x in along_x for z_lo in along_lo]
    received = lax.all_to_all(pieces, REP, 0, 0, axis_index_groups=[along_rep], tiled=True)
    me = (lax.axis_index("x") + n_x - from_x) % n_x * n_lo + (lax.axis_index("z_lo") + n_lo - from_lo) % n_lo
    own = lax.dynamic_slice(master, (me // across * SUBLANES, me % across * width), (SUBLANES, width))
    mean = jnp.sum(own[None] - received.astype(jnp.float32), axis=0) / replicas
    copies = jnp.broadcast_to(mean[None], (n_lo,) + mean.shape)
    column = lax.all_to_all(copies, "z_lo", 0, 0, axis_index_groups=[along_lo], tiled=True)
    groups = near_groups()
    members = len(groups[0])
    vmem = pl.BlockSpec(memory_space=pltpu.VMEM)
    shares = pl.pallas_call(
        squares_kernel,
        out_shape=jax.ShapeDtypeStruct((members, LANES), jnp.float32),
        in_specs=[vmem],
        out_specs=vmem,
        compiler_params=pltpu.CompilerParams(vmem_limit_bytes=4 << 20),
        cost_estimate=pl.CostEstimate(flops=2 * column.size, bytes_accessed=4 * column.size, transcendentals=0),
    )(column)
    shares = lax.all_to_all(shares.reshape(members, 1, LANES), NAMES, 0, 0, axis_index_groups=groups, tiled=True)
    gathered = lax.all_gather(column, "x", axis_index_groups=[along_x]).reshape(replicas, SUBLANES, width)
    whole = jax.ShapeDtypeStruct((rows, cols), jnp.float32)
    half = jax.ShapeDtypeStruct((rows, cols), jnp.bfloat16)
    hbm = pl.BlockSpec(memory_space=pl.ANY)
    return pl.pallas_call(
        lambda *refs: finish_kernel(element_count, *refs),
        out_shape=(whole, whole, half),
        in_specs=[vmem] * 4,
        out_specs=(hbm,) * 3,
        scratch_shapes=[
            pltpu.VMEM((rows, cols), jnp.float32),
            pltpu.VMEM((rows, cols), jnp.float32),
            pltpu.VMEM((rows, cols), jnp.bfloat16),
            pltpu.SemaphoreType.DMA((3, OUT_CHUNKS)),
        ],
        compiler_params=pltpu.CompilerParams(vmem_limit_bytes=16 << 20),
        cost_estimate=pl.CostEstimate(flops=8 * rows * cols, bytes_accessed=22 * rows * cols, transcendentals=0),
    )(shares.reshape(members, LANES), gathered, master, momentum)


def solution(mesh):
    fine = Mesh(mesh.devices.reshape(SIZES), NAMES)
    rows = P(FSDP, None)
    return jax.shard_map(
        shards,
        mesh=fine,
        in_specs=(P(REP, FSDP, None), rows, rows),
        out_specs=(rows, rows, rows),
        check_vma=False,
    )
```

time: 68.3 us -> 61.9 us (0.906)
  waiting for transfers between devices: 13.4 us -> 5.74 us
  starting transfers between devices: 27.3 us -> 33.5 us
  other arithmetic: 2.81 us -> 0.08 us
  local copies, waits for them, and re-layouts: 2.55 us -> 0.03 us
  Pallas kernels: 0 us -> 2.12 us
  blocking collectives: 20.6 us -> 19.4 us
  between operations: 1.42 us -> 0.67 us
    all_to_all x2, waiting for transfers between devices: 13.4 us -> 5.74 us  [the longest x1 5.01 us: shards(): lax.all_to_all(pieces, REP, 0, 0, axis_index_groups=[along_rep], tiled=True)]
    all_to_all x2, starting transfers between devices: 27.3 us -> 33.5 us  [the longest x1 23.7 us: shards(): lax.all_to_all(shares.reshape(members, 1, LANES), NAMES, 0, 0, axis_index...]
    pallas_call x0 -> x2, Pallas kernels: none -> 2.12 us  [the longest x1 1.44 us: shards(): pl.pallas_call(lambda *refs: finish_kernel(element_count, *refs), out_sha...]
    reduce_sum x2 -> x0, other arithmetic: 1.37 us -> none  [the longest x1 0.73 us: shards(): squares = jnp.sum(shares[:, 0, 0])]
    convert_element_type x1 -> x0, other arithmetic: 1.31 us -> none  [shards(): return (new_master, new_momentum, new_master.astype(jnp.bfloat16))]
    another operation x1 -> x0, local copies, waits for them, and re-layouts: 1.31 us -> none  [to_all(): copies = jnp.broadcast_to(piece[None], (size,) + piece.shape)]
    unnamed x4, local copies, waits for them, and re-layouts: 1.22 us -> 0.01 us
    all_to_all x1, blocking collectives: 7.93 us -> 7.09 us  [shards(): lax.all_to_all(copies, 'z_lo', 0, 0, axis_index_groups=[along_lo], tiled=...]
where the time goes in v3:
time: 61.9 us; the launch traced here: 61.5 us
  starting transfers between devices  33.5 us (54%)
  blocking collectives  19.4 us (31%)
  waiting for transfers between devices  5.74 us (9%)
  Pallas kernels  2.12 us (3%)
  between operations  0.67 us (1%)
    all_to_all x1, starting transfers between devices, shards(): lax.all_to_all(shares.reshape(members, 1, LANES), NAMES, 0, 0, axis_index...  23.7 us
    all_gather x1, blocking collectives, shards(): lax.all_gather(column, 'x', axis_index_groups=[along_x])  12.3 us
    all_to_all x1, starting transfers between devices, shards(): lax.all_to_all(pieces, REP, 0, 0, axis_index_groups=[along_rep], tiled=True)  9.86 us
    all_to_all x1, blocking collectives, shards(): lax.all_to_all(copies, 'z_lo', 0, 0, axis_index_groups=[along_lo], tiled=...  7.09 us
    all_to_all x1, waiting for transfers between devices, shards(): lax.all_to_all(pieces, REP, 0, 0, axis_index_groups=[along_rep], tiled=True)  5.01 us
    pallas_call x1, Pallas kernels, shards(): pl.pallas_call(lambda *refs: finish_kernel(element_count, *refs), out_sha...  1.44 us
  transfers between devices with their start and end apart: 2, of which 2 were waited for; matrix products, arithmetic and copies ran while one was open for 0% of the time, Pallas kernels for 0%

profile of v3, /device:TPU:1, one launch (start us, length us, event | category | flops | bytes accessed | tf_op | source)
XLA Modules:
  0.0 61.5 jit_solution(3937878285523845204)
XLA Ops:
  0.6 9.9 %all-to-all-start = ((bf16[16,8,1280]{2,1,0:T(8,128)(2,1)}), bf16[16,8,1280]{2,1,0:T(8,128)(2,1)S(1)}, u32[]{:S(2)}, u32[]{:S(2)}) async-start(bf16[16,8,1280]{2,1,0:T(8,128)(2,1)} %bitcast.10), calls=%async_computation | async-start | bytes 655360 | tf_op jit(solution)/shard_map/all_to_all | solution.py:104
  10.5 0.0 dynamic-slice-start
  10.5 5.0 %all-to-all-done = bf16[16,8,1280]{2,1,0:T(8,128)(2,1)S(1)} async-done(((bf16[16,8,1280]{2,1,0:T(8,128)(2,1)}), bf16[16,8,1280]{2,1,0:T(8,128)(2,1)S(1)}, u32[]{:S(2)}, u32[]{:S(2)}) %all-to-all-start) | async-done | bytes 327712 | tf_op jit(solution)/shard_map/all_to_all | solution.py:104
  15.5 0.0 dynamic-slice-done
  15.5 0.1 subtract_reduce_fusion
  15.6 0.0 copy-start.1
  15.6 7.1 %all_to_all.15.column_ref = f32[4,8,1280]{2,1,0:T(8,128)S(1)} all-to-all(f32[4,8,1280]{2,1,0:T(8,128)S(1)} %broadcast_in_dim.2), channel_id=1, replica_groups={{64,96,0,32},{65,97,1,33},{66,98,2,34},{67,99,3,35},{68,100,4,36},{69,1..., dimensions={0} | all-to-all | bytes 327680 | tf_op jit(solution)/shard_map/all_to_all | solution.py:109
  22.7 0.0 copy-start
  22.7 0.7 %shard_map.58 = f32[128,128]{1,0:T(8,128)} custom-call(f32[4,8,1280]{2,1,0:T(8,128)S(1)} %all_to_all.15.column_ref), custom_call_target="tpu_custom_call" | custom-call | flops 81920 | bytes 163840 | tf_op jit(solution)/shard_map/pallas_call | solution.py:113
  23.4 23.7 %all-to-all-start.2 = ((f32[128,1,128]{2,1,0:T(1,128)}), f32[128,1,128]{2,1,0:T(1,128)S(1)}, u32[]{:S(2)}, u32[]{:S(2)}) async-start(f32[128,1,128]{2,1,0:T(1,128)} %bitcast.4), calls=%async_computation.2 | async-start | bytes 131072 | tf_op jit(solution)/shard_map/all_to_all | solution.py:121
  47.1 12.3 %all-gather.refs_1_ = f32[16,8,1280]{2,1,0:T(8,128)S(1)} all-gather(f32[4,8,1280]{2,1,0:T(8,128)S(1)} %all_to_all.15.column_ref), channel_id=2, replica_groups={{256,384,0,128},{257,385,1,129},{258,386,2,130},{259,387,3,131},{260,38..., dimensions={0}, use_global_device_ids=true | all-gather | bytes 819200 | tf_op jit(solution)/shard_map/all_gather | solution.py:122
  59.4 0.7 %all-to-all-done.2 = f32[128,1,128]{2,1,0:T(1,128)S(1)} async-done(((f32[128,1,128]{2,1,0:T(1,128)}), f32[128,1,128]{2,1,0:T(1,128)S(1)}, u32[]{:S(2)}, u32[]{:S(2)}) %all-to-all-start.2) | async-done | bytes 65568 | tf_op jit(solution)/shard_map/all_to_all | solution.py:121
  60.1 0.0 copy-done.1
  60.1 0.0 copy-done
  60.1 1.4 %shard_map.59 = (f32[16,10240]{1,0:T(8,128)}, f32[16,10240]{1,0:T(8,128)}, bf16[16,10240]{1,0:T(8,128)(2,1)}) custom-call(f32[128,128]{1,0:T(8,128)S(1)} %bitcast.9, f32[16,8,1280]{2,1,0:T(8,128)S(1)} %all-gather.refs_1_, f32[16,10240]{1,0:T(8,128)S(1)} %copy-done, f32[16,10240]{1,0:T(8,128)S(1)} %copy-done.1), custom_call_target="tpu_custom_call" | custom-call | flops 1310720 | bytes 3604480 | tf_op jit(solution)/shard_map/pallas_call | solution.py:126
  (2 shorter events, 0.0 us)
Async XLA Ops:
  0.6 14.9 %all-to-all-start = ((bf16[16,8,1280]{2,1,0:T(8,128)(2,1)}), bf16[16,8,1280]{2,1,0:T(8,128)(2,1)S(1)}, u32[]{:S(2)}, u32[]{:S(2)}) async-start(bf16[16,8,1280]{2,1,0:T(8,128)(2,1)} %bitcast.10), calls=%async_computation | async-start | bytes 655360 | tf_op jit(solution)/shard_map/all_to_all | solution.py:104
  10.5 5.0 %dynamic-slice-start = ((f32[16,10240]{1,0:T(8,128)}, s32[]{:T(128)}, s32[]{:T(128)}), f32[8,1280]{1,0:T(8,128)S(1)}, s32[]{:S(2)}) async-start(f32[16,10240]{1,0:T(8,128)} %refs_2_.1, s32[]{:T(128)} %select_n.28, s32[]{:T(128)} %select_n.30), calls=%async_computation.3 | async-start | bytes 82432 | tf_op jit(solution)/shard_map/dynamic_slice | solution.py:106
  15.6 44.5 %copy-start.1 = (f32[16,10240]{1,0:T(8,128)S(1)}, f32[16,10240]{1,0:T(8,128)}, u32[]{:S(2)}) copy-start(f32[16,10240]{1,0:T(8,128)} %refs_3_.1) | copy-start | bytes 1966084
  22.7 37.4 %copy-start = (f32[16,10240]{1,0:T(8,128)S(1)}, f32[16,10240]{1,0:T(8,128)}, u32[]{:S(2)}) copy-start(f32[16,10240]{1,0:T(8,128)} %refs_2_.1) | copy-start | bytes 1966084
  23.4 36.7 %all-to-all-start.2 = ((f32[128,1,128]{2,1,0:T(1,128)}), f32[128,1,128]{2,1,0:T(1,128)S(1)}, u32[]{:S(2)}, u32[]{:S(2)}) async-start(f32[128,1,128]{2,1,0:T(1,128)} %bitcast.4), calls=%async_computation.2 | async-start | bytes 131072 | tf_op jit(solution)/shard_map/all_to_all | solution.py:121

commit v4 on v3

--- a/solution.py
+++ b/solution.py
@@ -15,7 +15,9 @@
 SUBLANES = 8
 OUT_CHUNKS = 4
 PIECE_START = (2, 2)
-SHARE_START = (0, 0, 3)
+SHARE_START = (2, 3)
+TOP = 14
+FLOOR = 2.0**-100
 
 
 def turned(size, start):
@@ -29,39 +31,61 @@
     return place
 
 
-def near_groups():
+def near_groups(pairs):
     n_x, n_lo, n_y, n_hi, n_core = SIZES
-    from_x, from_y, from_hi = SHARE_START
+    from_y, from_hi = SHARE_START
     return [
         [
             position(x, (z_lo + n_lo // 2 * (z_hi * 2 // n_hi)) % n_lo, y, z_hi, core)
-            for x in turned(n_x, from_x)
+            for x in pair
             for y in turned(n_y, from_y)
             for z_hi in turned(n_hi, from_hi)
             for core in range(n_core)
         ]
+        for pair in pairs
         for z_lo in range(n_lo)
     ]
 
 
-def squares_kernel(column_ref, shares_ref):
-    pieces, _, width = column_ref.shape
+def blocks(width):
+    return [slice(start, start + LANES) for start in range(0, width, LANES)]
+
+
+def encode(piece):
+    parts = [piece[:, at] for at in blocks(piece.shape[1])]
+    largest = jnp.full_like(parts[0], FLOOR)
+    for part in parts:
+        largest = jnp.maximum(largest, jnp.abs(part))
+    exponent = jnp.ceil(jnp.log2(largest))
+    power = jnp.exp2(TOP - exponent)
+    return jnp.concatenate([part * power for part in parts] + [exponent], axis=1).astype(jnp.float16)
+
+
+def power_of(coded_ref, piece, width):
+    return jnp.exp2(coded_ref[piece, :, width : width + LANES] - TOP)
+
+
+def squares_kernel(coded_ref, shares_ref):
+    pieces, _, coded_width = coded_ref.shape
+    width = coded_width - LANES
     total = jnp.zeros((SUBLANES, LANES), jnp.float32)
     for piece in range(pieces):
-        for start in range(0, width, LANES):
-            value = column_ref[piece, :, start : start + LANES]
+        power = power_of(coded_ref, piece, width)
+        for at in blocks(width):
+            value = coded_ref[piece, :, at] * power
             total = total + value * value
     lanes = jnp.sum(total, axis=0, keepdims=True)
     shares_ref[...] = jnp.broadcast_to(lanes, shares_ref.shape)
 
 
 def finish_kernel(
-    element_count, shares_ref, pseudo_ref, master_ref, momentum_ref,
+    element_count, shares_ref, coded_ref, kept_ref, base_ref,
     new_master_ref, new_momentum_ref, working_ref,
     master_slot, momentum_slot, working_slot, sems,
 ):
-    pieces, _, width = pseudo_ref.shape
-    rows, cols = master_ref.shape
+    pieces, _, coded_width = coded_ref.shape
+    width = coded_width - LANES
+    rows, cols = kept_ref.shape
     bands = rows // SUBLANES
     across = pieces // bands
     squares = jnp.sum(shares_ref[...], keepdims=True)
@@ -69,14 +93,17 @@
     copies = []
     chunk = cols // OUT_CHUNKS
     for block in range(across):
-        at = slice(block * width, (block + 1) * width)
-        pseudo = jnp.concatenate([pseudo_ref[band * across + block] for band in range(bands)], axis=0)
-        clipped = factor * pseudo
-        new_momentum = 0.9 * momentum_ref[:, at] + clipped
-        new_master = master_ref[:, at] - 0.7 * (clipped + 0.9 * new_momentum)
-        momentum_slot[:, at] = new_momentum
-        master_slot[:, at] = new_master
-        working_slot[:, at] = new_master.astype(jnp.bfloat16)
+        own = [band * across + block for band in range(bands)]
+        powers = [power_of(coded_ref, piece, width) for piece in own]
+        for part in blocks(width):
+            at = slice(block * width + part.start, block * width + part.stop)
+            pseudo = jnp.concatenate([coded_ref[piece, :, part] * power for piece, power in zip(own, powers)], axis=0)
+            clipped = factor * pseudo
+            new_momentum = kept_ref[:, at] + clipped
+            new_master = base_ref[:, at] - 1.33 * clipped
+            momentum_slot[:, at] = new_momentum
+            master_slot[:, at] = new_master
+            working_slot[:, at] = new_master.astype(jnp.bfloat16)
         done = (block + 1) * width
         if done % chunk == 0:
             part = slice(done - chunk, done)
@@ -105,9 +132,16 @@
     me = (lax.axis_index("x") + n_x - from_x) % n_x * n_lo + (lax.axis_index("z_lo") + n_lo - from_lo) % n_lo
     own = lax.dynamic_slice(master, (me // across * SUBLANES, me % across * width), (SUBLANES, width))
     mean = jnp.sum(own[None] - received.astype(jnp.float32), axis=0) / replicas
-    copies = jnp.broadcast_to(mean[None], (n_lo,) + mean.shape)
-    column = lax.all_to_all(copies, "z_lo", 0, 0, axis_index_groups=[along_lo], tiled=True)
-    groups = near_groups()
+    kept = 0.9 * momentum
+    base = master - 0.63 * kept
+    mean, kept, base = lax.optimization_barrier((mean, kept, base))
+    coded = encode(mean)
+    near = replicas // bands
+    copies = jnp.broadcast_to(coded[None], (near,) + coded.shape)
+    firsts = [along_rep[start : start + near] for start in range(0, replicas, near)]
+    band = lax.all_to_all(copies, REP, 0, 0, axis_index_groups=firsts, tiled=True)
+    seconds = [[along_x[step], along_x[n_x - 1 - step]] for step in range(bands)]
+    groups = near_groups(seconds)
     members = len(groups[0])
     vmem = pl.BlockSpec(memory_space=pltpu.VMEM)
     shares = pl.pallas_call(
@@ -116,10 +150,10 @@
         in_specs=[vmem],
         out_specs=vmem,
         compiler_params=pltpu.CompilerParams(vmem_limit_bytes=4 << 20),
-        cost_estimate=pl.CostEstimate(flops=2 * column.size, bytes_accessed=4 * column.size, transcendentals=0),
-    )(column)
+        cost_estimate=pl.CostEstimate(flops=3 * band.size, bytes_accessed=4 * band.size, transcendentals=0),
+    )(band.astype(jnp.float32))
     shares = lax.all_to_all(shares.reshape(members, 1, LANES), NAMES, 0, 0, axis_index_groups=groups, tiled=True)
-    gathered = lax.all_gather(column, "x", axis_index_groups=[along_x]).reshape(replicas, SUBLANES, width)
+    gathered = lax.all_gather(band, "x", axis_index_groups=seconds).reshape(replicas, SUBLANES, width + LANES).astype(jnp.float32)
     whole = jax.ShapeDtypeStruct((rows, cols), jnp.float32)
     half = jax.ShapeDtypeStruct((rows, cols), jnp.bfloat16)
     hbm = pl.BlockSpec(memory_space=pl.ANY)
@@ -136,7 +170,7 @@
         ],
         compiler_params=pltpu.CompilerParams(vmem_limit_bytes=16 << 20),
         cost_estimate=pl.CostEstimate(flops=8 * rows * cols, bytes_accessed=22 * rows * cols, transcendentals=0),
-    )(shares.reshape(members, LANES), gathered, master, momentum)
+    )(shares.reshape(members, LANES), gathered, kept, base)
 
 
 def solution(mesh):

time: 61.9 us -> 59.2 us (0.956)
  blocking collectives: 19.4 us -> 16.4 us
  waiting for transfers between devices: 5.74 us -> 3.79 us
  other arithmetic: 0.08 us -> 1.55 us
  starting transfers between devices: 33.5 us -> 34.3 us
    all_gather x1, blocking collectives: 12.3 us -> 7.84 us  [shards(): lax.all_gather(band, 'x', axis_index_groups=seconds)]
    all_to_all x1, blocking collectives: 7.09 us -> 8.56 us  [shards(): lax.all_to_all(copies, REP, 0, 0, axis_index_groups=firsts, tiled=True)]
    all_to_all x1, waiting for transfers between devices: 5.01 us -> 3.78 us  [shards(): lax.all_to_all(pieces, REP, 0, 0, axis_index_groups=[along_rep], tiled=True)]
    sub x0 -> x1, other arithmetic: none -> 1.21 us  [shards(): base = master - 0.63 * kept]
    all_to_all x1, waiting for transfers between devices: 0.73 us -> 0.01 us  [shards(): lax.all_to_all(shares.reshape(members, 1, LANES), NAMES, 0, 0, axis_index...]
  transfers between devices with their start and end apart: 2 -> 2, of which waited for: 2 -> 1; matrix products, arithmetic and copies ran while one was open for 0% -> 2% of each run, Pallas kernels for 0% -> 0%
where the time goes in v4:
time: 59.2 us; the launch traced here: 58.9 us
  starting transfers between devices  34.3 us (58%)
  blocking collectives  16.4 us (28%)
  waiting for transfers between devices  3.79 us (6%)
  Pallas kernels  2.14 us (4%)
  other arithmetic  1.55 us (3%)
  between operations  0.73 us (1%)
    all_to_all x1, starting transfers between devices, shards(): lax.all_to_all(shares.reshape(members, 1, LANES), NAMES, 0, 0, axis_index...  24.3 us
    all_to_all x1, starting transfers between devices, shards(): lax.all_to_all(pieces, REP, 0, 0, axis_index_groups=[along_rep], tiled=True)  9.99 us
    all_to_all x1, blocking collectives, shards(): lax.all_to_all(copies, REP, 0, 0, axis_index_groups=firsts, tiled=True)  8.56 us
    all_gather x1, blocking collectives, shards(): lax.all_gather(band, 'x', axis_index_groups=seconds)  7.84 us
    all_to_all x1, waiting for transfers between devices, shards(): lax.all_to_all(pieces, REP, 0, 0, axis_index_groups=[along_rep], tiled=True)  3.78 us
    pallas_call x1, Pallas kernels, shards(): pl.pallas_call(lambda *refs: finish_kernel(element_count, *refs), out_sha...  1.42 us
    sub x1, other arithmetic, shards(): base = master - 0.63 * kept  1.21 us
  transfers between devices with their start and end apart: 2, of which 1 were waited for; matrix products, arithmetic and copies ran while one was open for 2% of the time, Pallas kernels for 0%

profile of v4, /device:TPU:1, one launch (start us, length us, event | category | flops | bytes accessed | tf_op | source)
XLA Modules:
  0.0 58.9 jit_solution(15729123997372807222)
XLA Ops:
  0.6 0.0 copy-start
  0.6 10.0 %all-to-all-start = ((bf16[16,8,1280]{2,1,0:T(8,128)(2,1)}), bf16[16,8,1280]{2,1,0:T(8,128)(2,1)S(1)}, u32[]{:S(2)}, u32[]{:S(2)}) async-start(bf16[16,8,1280]{2,1,0:T(8,128)(2,1)} %bitcast.10), calls=%async_computation | async-start | bytes 655360 | tf_op jit(solution)/shard_map/all_to_all | solution.py:131
  10.6 0.0 copy-done
  10.6 0.0 dynamic-slice-start
  10.6 1.2 %multiply_subtract_fusion = (f32[16,10240]{1,0:T(8,128)S(1)}, f32[16,10240]{1,0:T(8,128)S(1)}) fusion(f32[16,10240]{1,0:T(8,128)S(1)} %copy-done, f32[16,10240]{1,0:T(8,128)} %param.5), kind=kLoop, calls=%fused_computation | loop fusion | flops 491520 | bytes 2621440 | tf_op jit(solution)/shard_map/sub | solution.py:136
  11.9 3.8 %all-to-all-done = bf16[16,8,1280]{2,1,0:T(8,128)(2,1)S(1)} async-done(((bf16[16,8,1280]{2,1,0:T(8,128)(2,1)}), bf16[16,8,1280]{2,1,0:T(8,128)(2,1)S(1)}, u32[]{:S(2)}, u32[]{:S(2)}) %all-to-all-start) | async-done | bytes 327712 | tf_op jit(solution)/shard_map/all_to_all | solution.py:131
  15.6 0.0 dynamic-slice-done
  15.7 0.1 subtract_reduce_fusion
  16.0 8.6 %all_to_all.15 = f16[8,8,1408]{2,1,0:T(8,128)(2,1)S(1)} all-to-all(f16[8,8,1408]{2,1,0:T(8,128)(2,1)S(1)} %broadcast_in_dim.5), channel_id=1, replica_groups={{320,352,256,288,448,480,384,416},{64,96,0,32,192,224,128,160},{321,353..., dimensions={0} | all-to-all | bytes 360448 | tf_op jit(solution)/shard_map/all_to_all | solution.py:142
  24.6 0.7 %shard_map.58 = f32[64,128]{1,0:T(8,128)} custom-call(f32[8,8,1408]{2,1,0:T(8,128)S(1)} %convert_element_type.17.coded_ref), custom_call_target="tpu_custom_call" | custom-call | flops 270336 | bytes 360448 | tf_op jit(solution)/shard_map/pallas_call | solution.py:147
  25.3 24.3 %all-to-all-start.2 = ((f32[64,1,128]{2,1,0:T(1,128)}), f32[64,1,128]{2,1,0:T(1,128)S(1)}, u32[]{:S(2)}, u32[]{:S(2)}) async-start(f32[64,1,128]{2,1,0:T(1,128)} %bitcast.4), calls=%async_computation.2 | async-start | bytes 65536 | tf_op jit(solution)/shard_map/all_to_all | solution.py:155
  49.6 7.8 %all-gather = f16[16,8,1408]{2,1,0:T(8,128)(2,1)S(1)} all-gather(f16[8,8,1408]{2,1,0:T(8,128)(2,1)S(1)} %all_to_all.15), channel_id=2, replica_groups={{256,128},{384,0},{257,129},{385,1},{258,130},{386,2},{259,131},{387,3}..., dimensions={0}, use_global_device_ids=true | all-gather | bytes 540672 | tf_op jit(solution)/shard_map/all_gather | solution.py:156
  57.5 0.0 all-to-all-done.2
  57.5 1.4 %shard_map.59 = (f32[16,10240]{1,0:T(8,128)}, f32[16,10240]{1,0:T(8,128)}, bf16[16,10240]{1,0:T(8,128)(2,1)}) custom-call(f32[64,128]{1,0:T(8,128)S(1)} %bitcast.9, f32[16,8,1408]{2,1,0:T(8,128)S(1)} %convert_element_type.21.refs_1_, f32[16,10240]{1,0:T(8,128)S(1)} %get-tuple-element.7.refs_2_, f32[16,10240]{1,0:T(8,128)S(1)} %get-tuple-element.8.refs_3_), custom_call_target="tpu_custom_call" | custom-call | flops 1310720 | bytes 3604480 | tf_op jit(solution)/shard_map/pallas_call | solution.py:160
  (15 shorter events, 0.3 us)
Async XLA Ops:
  0.6 10.0 %copy-start = (f32[16,10240]{1,0:T(8,128)S(1)}, f32[16,10240]{1,0:T(8,128)}, u32[]{:S(2)}) copy-start(f32[16,10240]{1,0:T(8,128)} %param.4) | copy-start | bytes 1966084
  0.6 15.0 %all-to-all-start = ((bf16[16,8,1280]{2,1,0:T(8,128)(2,1)}), bf16[16,8,1280]{2,1,0:T(8,128)(2,1)S(1)}, u32[]{:S(2)}, u32[]{:S(2)}) async-start(bf16[16,8,1280]{2,1,0:T(8,128)(2,1)} %bitcast.10), calls=%async_computation | async-start | bytes 655360 | tf_op jit(solution)/shard_map/all_to_all | solution.py:131
  10.6 5.0 %dynamic-slice-start = ((f32[16,10240]{1,0:T(8,128)}, s32[]{:T(128)}, s32[]{:T(128)}), f32[8,1280]{1,0:T(8,128)S(1)}, s32[]{:S(2)}) async-start(f32[16,10240]{1,0:T(8,128)} %param.4, s32[]{:T(128)} %select_n.28, s32[]{:T(128)} %select_n.30), calls=%async_computation.3 | async-start | bytes 82432 | tf_op jit(solution)/shard_map/dynamic_slice | solution.py:133
  25.3 32.2 %all-to-all-start.2 = ((f32[64,1,128]{2,1,0:T(1,128)}), f32[64,1,128]{2,1,0:T(1,128)S(1)}, u32[]{:S(2)}, u32[]{:S(2)}) async-start(f32[64,1,128]{2,1,0:T(1,128)} %bitcast.4), calls=%async_computation.2 | async-start | bytes 65536 | tf_op jit(solution)/shard_map/all_to_all | solution.py:155

commit v5 on v4

--- a/solution.py
+++ b/solution.py
@@ -37,7 +37,7 @@
     return [
         [
             position(x, (z_lo + n_lo // 2 * (z_hi * 2 // n_hi)) % n_lo, y, z_hi, core)
-            for x in pair
+            for x in sorted(pair)
             for y in turned(n_y, from_y)
             for z_hi in turned(n_hi, from_hi)
             for core in range(n_core)
@@ -88,7 +88,8 @@
     rows, cols = kept_ref.shape
     bands = rows // SUBLANES
     across = pieces // bands
-    squares = jnp.sum(shares_ref[...], keepdims=True)
+    half = shares_ref.shape[0] // 2
+    squares = jnp.sum(shares_ref[:half], keepdims=True) + jnp.sum(shares_ref[half:], keepdims=True)
     factor = jnp.minimum(1.0, 0.5 * math.sqrt(element_count) * lax.rsqrt(squares + 1e-06))
     copies = []
     chunk = cols // OUT_CHUNKS

time: 59.2 us -> 58 us (0.980)
  starting transfers between devices: 34.3 us -> 32 us
  waiting for transfers between devices: 3.79 us -> 5.05 us
    all_to_all x1, starting transfers between devices: 24.3 us -> 22 us  [shards(): lax.all_to_all(shares.reshape(members, 1, LANES), NAMES, 0, 0, axis_index...]
    all_to_all x1, waiting for transfers between devices: 0.01 us -> 1.27 us  [shards(): lax.all_to_all(shares.reshape(members, 1, LANES), NAMES, 0, 0, axis_index...]
  transfers between devices with their start and end apart: 2 -> 2, of which waited for: 1 -> 2; matrix products, arithmetic and copies ran while one was open for 2% -> 2% of each run, Pallas kernels for 0% -> 0%
where the time goes in v5:
time: 58 us; the launch traced here: 57.7 us
  starting transfers between devices  32 us (55%)
  blocking collectives  16.2 us (28%)
  waiting for transfers between devices  5.05 us (9%)
  Pallas kernels  2.14 us (4%)
  other arithmetic  1.55 us (3%)
  between operations  0.72 us (1%)
    all_to_all x1, starting transfers between devices, shards(): lax.all_to_all(shares.reshape(members, 1, LANES), NAMES, 0, 0, axis_index...  22 us
    all_to_all x1, starting transfers between devices, shards(): lax.all_to_all(pieces, REP, 0, 0, axis_index_groups=[along_rep], tiled=True)  9.99 us
    all_to_all x1, blocking collectives, shards(): lax.all_to_all(copies, REP, 0, 0, axis_index_groups=firsts, tiled=True)  8.56 us
    all_gather x1, blocking collectives, shards(): lax.all_gather(band, 'x', axis_index_groups=seconds)  7.66 us
    all_to_all x1, waiting for transfers between devices, shards(): lax.all_to_all(pieces, REP, 0, 0, axis_index_groups=[along_rep], tiled=True)  3.78 us
    pallas_call x1, Pallas kernels, shards(): pl.pallas_call(lambda *refs: finish_kernel(element_count, *refs), out_sha...  1.42 us
    all_to_all x1, waiting for transfers between devices, shards(): lax.all_to_all(shares.reshape(members, 1, LANES), NAMES, 0, 0, axis_index...  1.27 us
    sub x1, other arithmetic, shards(): base = master - 0.63 * kept  1.21 us
  transfers between devices with their start and end apart: 2, of which 2 were waited for; matrix products, arithmetic and copies ran while one was open for 2% of the time, Pallas kernels for 0%

profile of v5, /device:TPU:1, one launch (start us, length us, event | category | flops | bytes accessed | tf_op | source)
XLA Modules:
  0.0 57.7 jit_solution(11900160954964192769)
XLA Ops:
  0.6 0.0 copy-start
  0.6 10.0 %all-to-all-start = ((bf16[16,8,1280]{2,1,0:T(8,128)(2,1)}), bf16[16,8,1280]{2,1,0:T(8,128)(2,1)S(1)}, u32[]{:S(2)}, u32[]{:S(2)}) async-start(bf16[16,8,1280]{2,1,0:T(8,128)(2,1)} %bitcast.10), calls=%async_computation | async-start | bytes 655360 | tf_op jit(solution)/shard_map/all_to_all | solution.py:132
  10.6 0.0 copy-done
  10.6 0.0 dynamic-slice-start
  10.6 1.2 %multiply_subtract_fusion = (f32[16,10240]{1,0:T(8,128)S(1)}, f32[16,10240]{1,0:T(8,128)S(1)}) fusion(f32[16,10240]{1,0:T(8,128)S(1)} %copy-done, f32[16,10240]{1,0:T(8,128)} %param.5), kind=kLoop, calls=%fused_computation | loop fusion | flops 491520 | bytes 2621440 | tf_op jit(solution)/shard_map/sub | solution.py:137
  11.9 3.8 %all-to-all-done = bf16[16,8,1280]{2,1,0:T(8,128)(2,1)S(1)} async-done(((bf16[16,8,1280]{2,1,0:T(8,128)(2,1)}), bf16[16,8,1280]{2,1,0:T(8,128)(2,1)S(1)}, u32[]{:S(2)}, u32[]{:S(2)}) %all-to-all-start) | async-done | bytes 327712 | tf_op jit(solution)/shard_map/all_to_all | solution.py:132
  15.6 0.0 dynamic-slice-done
  15.7 0.1 subtract_reduce_fusion
  16.0 8.6 %all_to_all.15 = f16[8,8,1408]{2,1,0:T(8,128)(2,1)S(1)} all-to-all(f16[8,8,1408]{2,1,0:T(8,128)(2,1)S(1)} %broadcast_in_dim.5), channel_id=1, replica_groups={{320,352,256,288,448,480,384,416},{64,96,0,32,192,224,128,160},{321,353..., dimensions={0} | all-to-all | bytes 360448 | tf_op jit(solution)/shard_map/all_to_all | solution.py:143
  24.6 0.7 %shard_map.58 = f32[64,128]{1,0:T(8,128)} custom-call(f32[8,8,1408]{2,1,0:T(8,128)S(1)} %convert_element_type.17.coded_ref), custom_call_target="tpu_custom_call" | custom-call | flops 270336 | bytes 360448 | tf_op jit(solution)/shard_map/pallas_call | solution.py:148
  25.3 22.0 %all-to-all-start.2 = ((f32[64,1,128]{2,1,0:T(1,128)}), f32[64,1,128]{2,1,0:T(1,128)S(1)}, u32[]{:S(2)}, u32[]{:S(2)}) async-start(f32[64,1,128]{2,1,0:T(1,128)} %bitcast.4), calls=%async_computation.2 | async-start | bytes 65536 | tf_op jit(solution)/shard_map/all_to_all | solution.py:156
  47.3 7.7 %all-gather = f16[16,8,1408]{2,1,0:T(8,128)(2,1)S(1)} all-gather(f16[8,8,1408]{2,1,0:T(8,128)(2,1)S(1)} %all_to_all.15), channel_id=2, replica_groups={{256,128},{384,0},{257,129},{385,1},{258,130},{386,2},{259,131},{387,3}..., dimensions={0}, use_global_device_ids=true | all-gather | bytes 540672 | tf_op jit(solution)/shard_map/all_gather | solution.py:157
  55.0 1.3 %all-to-all-done.2 = f32[64,1,128]{2,1,0:T(1,128)S(1)} async-done(((f32[64,1,128]{2,1,0:T(1,128)}), f32[64,1,128]{2,1,0:T(1,128)S(1)}, u32[]{:S(2)}, u32[]{:S(2)}) %all-to-all-start.2) | async-done | bytes 32800 | tf_op jit(solution)/shard_map/all_to_all | solution.py:156
  56.3 1.4 %shard_map.59 = (f32[16,10240]{1,0:T(8,128)}, f32[16,10240]{1,0:T(8,128)}, bf16[16,10240]{1,0:T(8,128)(2,1)}) custom-call(f32[64,128]{1,0:T(8,128)S(1)} %bitcast.9, f32[16,8,1408]{2,1,0:T(8,128)S(1)} %convert_element_type.21.refs_1_, f32[16,10240]{1,0:T(8,128)S(1)} %get-tuple-element.7.refs_2_, f32[16,10240]{1,0:T(8,128)S(1)} %get-tuple-element.8.refs_3_), custom_call_target="tpu_custom_call" | custom-call | flops 1310720 | bytes 3604480 | tf_op jit(solution)/shard_map/pallas_call | solution.py:161
  (15 shorter events, 0.3 us)
Async XLA Ops:
  0.6 10.0 %copy-start = (f32[16,10240]{1,0:T(8,128)S(1)}, f32[16,10240]{1,0:T(8,128)}, u32[]{:S(2)}) copy-start(f32[16,10240]{1,0:T(8,128)} %param.4) | copy-start | bytes 1966084
  0.6 15.0 %all-to-all-start = ((bf16[16,8,1280]{2,1,0:T(8,128)(2,1)}), bf16[16,8,1280]{2,1,0:T(8,128)(2,1)S(1)}, u32[]{:S(2)}, u32[]{:S(2)}) async-start(bf16[16,8,1280]{2,1,0:T(8,128)(2,1)} %bitcast.10), calls=%async_computation | async-start | bytes 655360 | tf_op jit(solution)/shard_map/all_to_all | solution.py:132
  10.6 5.0 %dynamic-slice-start = ((f32[16,10240]{1,0:T(8,128)}, s32[]{:T(128)}, s32[]{:T(128)}), f32[8,1280]{1,0:T(8,128)S(1)}, s32[]{:S(2)}) async-start(f32[16,10240]{1,0:T(8,128)} %param.4, s32[]{:T(128)} %select_n.28, s32[]{:T(128)} %select_n.30), calls=%async_computation.3 | async-start | bytes 82432 | tf_op jit(solution)/shard_map/dynamic_slice | solution.py:134
  25.3 31.0 %all-to-all-start.2 = ((f32[64,1,128]{2,1,0:T(1,128)}), f32[64,1,128]{2,1,0:T(1,128)S(1)}, u32[]{:S(2)}, u32[]{:S(2)}) async-start(f32[64,1,128]{2,1,0:T(1,128)} %bitcast.4), calls=%async_computation.2 | async-start | bytes 65536 | tf_op jit(solution)/shard_map/all_to_all | solution.py:156

commit v6 on v5

--- a/solution.py
+++ b/solution.py
@@ -14,7 +14,7 @@
 LANES = 128
 SUBLANES = 8
 OUT_CHUNKS = 4
-PIECE_START = (2, 2)
+PIECE_START = (3, 2)
 SHARE_START = (2, 3)
 TOP = 14
 FLOOR = 2.0**-100

time: 58 us -> 56.8 us (0.979)
  starting transfers between devices: 32 us -> 31.2 us
    all_gather x1, blocking collectives: 7.66 us -> 6.45 us  [shards(): lax.all_gather(band, 'x', axis_index_groups=seconds)]
    all_to_all x1, starting transfers between devices: 22 us -> 21.2 us  [shards(): lax.all_to_all(shares.reshape(members, 1, LANES), NAMES, 0, 0, axis_index...]
    all_to_all x1, blocking collectives: 8.56 us -> 9.33 us  [shards(): lax.all_to_all(copies, REP, 0, 0, axis_index_groups=firsts, tiled=True)]
where the time goes in v6:
time: 56.8 us; the launch traced here: 56.5 us
  starting transfers between devices  31.2 us (55%)
  blocking collectives  15.8 us (28%)
  waiting for transfers between devices  5.07 us (9%)
  Pallas kernels  2.14 us (4%)
  other arithmetic  1.55 us (3%)
  between operations  0.72 us (1%)
    all_to_all x1, starting transfers between devices, shards(): lax.all_to_all(shares.reshape(members, 1, LANES), NAMES, 0, 0, axis_index...  21.2 us
    all_to_all x1, starting transfers between devices, shards(): lax.all_to_all(pieces, REP, 0, 0, axis_index_groups=[along_rep], tiled=True)  9.93 us
    all_to_all x1, blocking collectives, shards(): lax.all_to_all(copies, REP, 0, 0, axis_index_groups=firsts, tiled=True)  9.33 us
    all_gather x1, blocking collectives, shards(): lax.all_gather(band, 'x', axis_index_groups=seconds)  6.45 us
    all_to_all x1, waiting for transfers between devices, shards(): lax.all_to_all(pieces, REP, 0, 0, axis_index_groups=[along_rep], tiled=True)  3.8 us
    pallas_call x1, Pallas kernels, shards(): pl.pallas_call(lambda *refs: finish_kernel(element_count, *refs), out_sha...  1.42 us
    all_to_all x1, waiting for transfers between devices, shards(): lax.all_to_all(shares.reshape(members, 1, LANES), NAMES, 0, 0, axis_index...  1.27 us
    sub x1, other arithmetic, shards(): base = master - 0.63 * kept  1.21 us
  transfers between devices with their start and end apart: 2, of which 2 were waited for; matrix products, arithmetic and copies ran while one was open for 2% of the time, Pallas kernels for 0%

profile of v6, /device:TPU:1, one launch (start us, length us, event | category | flops | bytes accessed | tf_op | source)
XLA Modules:
  0.0 56.5 jit_solution(7253247460618540887)
XLA Ops:
  0.6 0.0 copy-start
  0.6 9.9 %all-to-all-start = ((bf16[16,8,1280]{2,1,0:T(8,128)(2,1)}), bf16[16,8,1280]{2,1,0:T(8,128)(2,1)S(1)}, u32[]{:S(2)}, u32[]{:S(2)}) async-start(bf16[16,8,1280]{2,1,0:T(8,128)(2,1)} %bitcast.10), calls=%async_computation | async-start | bytes 655360 | tf_op jit(solution)/shard_map/all_to_all | solution.py:132
  10.6 0.0 copy-done
  10.6 0.0 dynamic-slice-start
  10.6 1.2 %multiply_subtract_fusion = (f32[16,10240]{1,0:T(8,128)S(1)}, f32[16,10240]{1,0:T(8,128)S(1)}) fusion(f32[16,10240]{1,0:T(8,128)S(1)} %copy-done, f32[16,10240]{1,0:T(8,128)} %param.5), kind=kLoop, calls=%fused_computation | loop fusion | flops 491520 | bytes 2621440 | tf_op jit(solution)/shard_map/sub | solution.py:137
  11.8 3.8 %all-to-all-done = bf16[16,8,1280]{2,1,0:T(8,128)(2,1)S(1)} async-done(((bf16[16,8,1280]{2,1,0:T(8,128)(2,1)}), bf16[16,8,1280]{2,1,0:T(8,128)(2,1)S(1)}, u32[]{:S(2)}, u32[]{:S(2)}) %all-to-all-start) | async-done | bytes 327712 | tf_op jit(solution)/shard_map/all_to_all | solution.py:132
  15.6 0.0 dynamic-slice-done
  15.6 0.1 subtract_reduce_fusion
  16.0 9.3 %all_to_all.15 = f16[8,8,1408]{2,1,0:T(8,128)(2,1)S(1)} all-to-all(f16[8,8,1408]{2,1,0:T(8,128)(2,1)S(1)} %broadcast_in_dim.5), channel_id=1, replica_groups={{448,480,384,416,64,96,0,32},{192,224,128,160,320,352,256,288},{449,481..., dimensions={0} | all-to-all | bytes 360448 | tf_op jit(solution)/shard_map/all_to_all | solution.py:143
  25.3 0.7 %shard_map.58 = f32[64,128]{1,0:T(8,128)} custom-call(f32[8,8,1408]{2,1,0:T(8,128)S(1)} %convert_element_type.17.coded_ref), custom_call_target="tpu_custom_call" | custom-call | flops 270336 | bytes 360448 | tf_op jit(solution)/shard_map/pallas_call | solution.py:148
  26.0 21.2 %all-to-all-start.2 = ((f32[64,1,128]{2,1,0:T(1,128)}), f32[64,1,128]{2,1,0:T(1,128)S(1)}, u32[]{:S(2)}, u32[]{:S(2)}) async-start(f32[64,1,128]{2,1,0:T(1,128)} %bitcast.4), calls=%async_computation.2 | async-start | bytes 65536 | tf_op jit(solution)/shard_map/all_to_all | solution.py:156
  47.3 6.5 %all-gather = f16[16,8,1408]{2,1,0:T(8,128)(2,1)S(1)} all-gather(f16[8,8,1408]{2,1,0:T(8,128)(2,1)S(1)} %all_to_all.15), channel_id=2, replica_groups={{384,256},{0,128},{385,257},{1,129},{386,258},{2,130},{387,259},{3,131}..., dimensions={0}, use_global_device_ids=true | all-gather | bytes 540672 | tf_op jit(solution)/shard_map/all_gather | solution.py:157
  53.8 1.3 %all-to-all-done.2 = f32[64,1,128]{2,1,0:T(1,128)S(1)} async-done(((f32[64,1,128]{2,1,0:T(1,128)}), f32[64,1,128]{2,1,0:T(1,128)S(1)}, u32[]{:S(2)}, u32[]{:S(2)}) %all-to-all-start.2) | async-done | bytes 32800 | tf_op jit(solution)/shard_map/all_to_all | solution.py:156
  55.1 1.4 %shard_map.59 = (f32[16,10240]{1,0:T(8,128)}, f32[16,10240]{1,0:T(8,128)}, bf16[16,10240]{1,0:T(8,128)(2,1)}) custom-call(f32[64,128]{1,0:T(8,128)S(1)} %bitcast.9, f32[16,8,1408]{2,1,0:T(8,128)S(1)} %convert_element_type.21.refs_1_, f32[16,10240]{1,0:T(8,128)S(1)} %get-tuple-element.7.refs_2_, f32[16,10240]{1,0:T(8,128)S(1)} %get-tuple-element.8.refs_3_), custom_call_target="tpu_custom_call" | custom-call | flops 1310720 | bytes 3604480 | tf_op jit(solution)/shard_map/pallas_call | solution.py:161
  (15 shorter events, 0.3 us)
Async XLA Ops:
  0.6 9.9 %copy-start = (f32[16,10240]{1,0:T(8,128)S(1)}, f32[16,10240]{1,0:T(8,128)}, u32[]{:S(2)}) copy-start(f32[16,10240]{1,0:T(8,128)} %param.4) | copy-start | bytes 1966084
  0.6 15.0 %all-to-all-start = ((bf16[16,8,1280]{2,1,0:T(8,128)(2,1)}), bf16[16,8,1280]{2,1,0:T(8,128)(2,1)S(1)}, u32[]{:S(2)}, u32[]{:S(2)}) async-start(bf16[16,8,1280]{2,1,0:T(8,128)(2,1)} %bitcast.10), calls=%async_computation | async-start | bytes 655360 | tf_op jit(solution)/shard_map/all_to_all | solution.py:132
  10.6 5.0 %dynamic-slice-start = ((f32[16,10240]{1,0:T(8,128)}, s32[]{:T(128)}, s32[]{:T(128)}), f32[8,1280]{1,0:T(8,128)S(1)}, s32[]{:S(2)}) async-start(f32[16,10240]{1,0:T(8,128)} %param.4, s32[]{:T(128)} %select_n.28, s32[]{:T(128)} %select_n.30), calls=%async_computation.3 | async-start | bytes 82432 | tf_op jit(solution)/shard_map/dynamic_slice | solution.py:134
  26.0 29.0 %all-to-all-start.2 = ((f32[64,1,128]{2,1,0:T(1,128)}), f32[64,1,128]{2,1,0:T(1,128)S(1)}, u32[]{:S(2)}, u32[]{:S(2)}) async-start(f32[64,1,128]{2,1,0:T(1,128)} %bitcast.4), calls=%async_computation.2 | async-start | bytes 65536 | tf_op jit(solution)/shard_map/all_to_all | solution.py:156

commit v7 on v6

--- a/solution.py
+++ b/solution.py
@@ -37,7 +37,7 @@
     return [
         [
             position(x, (z_lo + n_lo // 2 * (z_hi * 2 // n_hi)) % n_lo, y, z_hi, core)
-            for x in sorted(pair)
+            for x in pair
             for y in turned(n_y, from_y)
             for z_hi in turned(n_hi, from_hi)
             for core in range(n_core)

time: 56.8 us -> 56.8 us (level)
  no operation moved by 1% of the time
where the time goes in v7:
time: 56.8 us; the launch traced here: 56.5 us
  starting transfers between devices  31.2 us (55%)
  blocking collectives  15.8 us (28%)
  waiting for transfers between devices  5.07 us (9%)
  Pallas kernels  2.14 us (4%)
  other arithmetic  1.55 us (3%)
  between operations  0.72 us (1%)
    all_to_all x1, starting transfers between devices, shards(): lax.all_to_all(shares.reshape(members, 1, LANES), NAMES, 0, 0, axis_index...  21.2 us
    all_to_all x1, starting transfers between devices, shards(): lax.all_to_all(pieces, REP, 0, 0, axis_index_groups=[along_rep], tiled=True)  9.93 us
    all_to_all x1, blocking collectives, shards(): lax.all_to_all(copies, REP, 0, 0, axis_index_groups=firsts, tiled=True)  9.33 us
    all_gather x1, blocking collectives, shards(): lax.all_gather(band, 'x', axis_index_groups=seconds)  6.45 us
    all_to_all x1, waiting for transfers between devices, shards(): lax.all_to_all(pieces, REP, 0, 0, axis_index_groups=[along_rep], tiled=True)  3.8 us
    pallas_call x1, Pallas kernels, shards(): pl.pallas_call(lambda *refs: finish_kernel(element_count, *refs), out_sha...  1.42 us
    all_to_all x1, waiting for transfers between devices, shards(): lax.all_to_all(shares.reshape(members, 1, LANES), NAMES, 0, 0, axis_index...  1.27 us
    sub x1, other arithmetic, shards(): base = master - 0.63 * kept  1.21 us
  transfers between devices with their start and end apart: 2, of which 2 were waited for; matrix products, arithmetic and copies ran while one was open for 2% of the time, Pallas kernels for 0%

profile of v7, /device:TPU:1, one launch (start us, length us, event | category | flops | bytes accessed | tf_op | source)
XLA Modules:
  0.0 56.5 jit_solution(13340824361150885473)
XLA Ops:
  0.6 0.0 copy-start
  0.6 9.9 %all-to-all-start = ((bf16[16,8,1280]{2,1,0:T(8,128)(2,1)}), bf16[16,8,1280]{2,1,0:T(8,128)(2,1)S(1)}, u32[]{:S(2)}, u32[]{:S(2)}) async-start(bf16[16,8,1280]{2,1,0:T(8,128)(2,1)} %bitcast.10), calls=%async_computation | async-start | bytes 655360 | tf_op jit(solution)/shard_map/all_to_all | solution.py:132
  10.6 0.0 copy-done
  10.6 0.0 dynamic-slice-start
  10.6 1.2 %multiply_subtract_fusion = (f32[16,10240]{1,0:T(8,128)S(1)}, f32[16,10240]{1,0:T(8,128)S(1)}) fusion(f32[16,10240]{1,0:T(8,128)S(1)} %copy-done, f32[16,10240]{1,0:T(8,128)} %param.5), kind=kLoop, calls=%fused_computation | loop fusion | flops 491520 | bytes 2621440 | tf_op jit(solution)/shard_map/sub | solution.py:137
  11.8 3.8 %all-to-all-done = bf16[16,8,1280]{2,1,0:T(8,128)(2,1)S(1)} async-done(((bf16[16,8,1280]{2,1,0:T(8,128)(2,1)}), bf16[16,8,1280]{2,1,0:T(8,128)(2,1)S(1)}, u32[]{:S(2)}, u32[]{:S(2)}) %all-to-all-start) | async-done | bytes 327712 | tf_op jit(solution)/shard_map/all_to_all | solution.py:132
  15.6 0.0 dynamic-slice-done
  15.6 0.1 subtract_reduce_fusion
  16.0 9.3 %all_to_all.15 = f16[8,8,1408]{2,1,0:T(8,128)(2,1)S(1)} all-to-all(f16[8,8,1408]{2,1,0:T(8,128)(2,1)S(1)} %broadcast_in_dim.5), channel_id=1, replica_groups={{448,480,384,416,64,96,0,32},{192,224,128,160,320,352,256,288},{449,481..., dimensions={0} | all-to-all | bytes 360448 | tf_op jit(solution)/shard_map/all_to_all | solution.py:143
  25.3 0.7 %shard_map.58 = f32[64,128]{1,0:T(8,128)} custom-call(f32[8,8,1408]{2,1,0:T(8,128)S(1)} %convert_element_type.17.coded_ref), custom_call_target="tpu_custom_call" | custom-call | flops 270336 | bytes 360448 | tf_op jit(solution)/shard_map/pallas_call | solution.py:148
  26.0 21.2 %all-to-all-start.2 = ((f32[64,1,128]{2,1,0:T(1,128)}), f32[64,1,128]{2,1,0:T(1,128)S(1)}, u32[]{:S(2)}, u32[]{:S(2)}) async-start(f32[64,1,128]{2,1,0:T(1,128)} %bitcast.4), calls=%async_computation.2 | async-start | bytes 65536 | tf_op jit(solution)/shard_map/all_to_all | solution.py:156
  47.3 6.5 %all-gather = f16[16,8,1408]{2,1,0:T(8,128)(2,1)S(1)} all-gather(f16[8,8,1408]{2,1,0:T(8,128)(2,1)S(1)} %all_to_all.15), channel_id=2, replica_groups={{384,256},{0,128},{385,257},{1,129},{386,258},{2,130},{387,259},{3,131}..., dimensions={0}, use_global_device_ids=true | all-gather | bytes 540672 | tf_op jit(solution)/shard_map/all_gather | solution.py:157
  53.8 1.3 %all-to-all-done.2 = f32[64,1,128]{2,1,0:T(1,128)S(1)} async-done(((f32[64,1,128]{2,1,0:T(1,128)}), f32[64,1,128]{2,1,0:T(1,128)S(1)}, u32[]{:S(2)}, u32[]{:S(2)}) %all-to-all-start.2) | async-done | bytes 32800 | tf_op jit(solution)/shard_map/all_to_all | solution.py:156
  55.1 1.4 %shard_map.59 = (f32[16,10240]{1,0:T(8,128)}, f32[16,10240]{1,0:T(8,128)}, bf16[16,10240]{1,0:T(8,128)(2,1)}) custom-call(f32[64,128]{1,0:T(8,128)S(1)} %bitcast.9, f32[16,8,1408]{2,1,0:T(8,128)S(1)} %convert_element_type.21.refs_1_, f32[16,10240]{1,0:T(8,128)S(1)} %get-tuple-element.7.refs_2_, f32[16,10240]{1,0:T(8,128)S(1)} %get-tuple-element.8.refs_3_), custom_call_target="tpu_custom_call" | custom-call | flops 1310720 | bytes 3604480 | tf_op jit(solution)/shard_map/pallas_call | solution.py:161
  (15 shorter events, 0.3 us)
Async XLA Ops:
  0.6 9.9 %copy-start = (f32[16,10240]{1,0:T(8,128)S(1)}, f32[16,10240]{1,0:T(8,128)}, u32[]{:S(2)}) copy-start(f32[16,10240]{1,0:T(8,128)} %param.4) | copy-start | bytes 1966084
  0.6 15.0 %all-to-all-start = ((bf16[16,8,1280]{2,1,0:T(8,128)(2,1)}), bf16[16,8,1280]{2,1,0:T(8,128)(2,1)S(1)}, u32[]{:S(2)}, u32[]{:S(2)}) async-start(bf16[16,8,1280]{2,1,0:T(8,128)(2,1)} %bitcast.10), calls=%async_computation | async-start | bytes 655360 | tf_op jit(solution)/shard_map/all_to_all | solution.py:132
  10.6 5.0 %dynamic-slice-start = ((f32[16,10240]{1,0:T(8,128)}, s32[]{:T(128)}, s32[]{:T(128)}), f32[8,1280]{1,0:T(8,128)S(1)}, s32[]{:S(2)}) async-start(f32[16,10240]{1,0:T(8,128)} %param.4, s32[]{:T(128)} %select_n.28, s32[]{:T(128)} %select_n.30), calls=%async_computation.3 | async-start | bytes 82432 | tf_op jit(solution)/shard_map/dynamic_slice | solution.py:134
  26.0 29.0 %all-to-all-start.2 = ((f32[64,1,128]{2,1,0:T(1,128)}), f32[64,1,128]{2,1,0:T(1,128)S(1)}, u32[]{:S(2)}, u32[]{:S(2)}) async-start(f32[64,1,128]{2,1,0:T(1,128)} %bitcast.4), calls=%async_computation.2 | async-start | bytes 65536 | tf_op jit(solution)/shard_map/all_to_all | solution.py:156

commit v8 on v6

--- a/solution.py
+++ b/solution.py
@@ -13,7 +13,7 @@
 FSDP = ("y", "z_hi", "core")
 LANES = 128
 SUBLANES = 8
-OUT_CHUNKS = 4
+OUT_CHUNKS = 8
 PIECE_START = (3, 2)
 SHARE_START = (2, 3)
 TOP = 14

time: 56.8 us -> 56.9 us (level)
  no operation moved by 1% of the time
where the time goes in v8:
time: 56.9 us; the launch traced here: 56.6 us
  starting transfers between devices  31.2 us (55%)
  blocking collectives  15.8 us (28%)
  waiting for transfers between devices  5.07 us (9%)
  Pallas kernels  2.22 us (4%)
  other arithmetic  1.55 us (3%)
  between operations  0.72 us (1%)
    all_to_all x1, starting transfers between devices, shards(): lax.all_to_all(shares.reshape(members, 1, LANES), NAMES, 0, 0, axis_index...  21.2 us
    all_to_all x1, starting transfers between devices, shards(): lax.all_to_all(pieces, REP, 0, 0, axis_index_groups=[along_rep], tiled=True)  9.93 us
    all_to_all x1, blocking collectives, shards(): lax.all_to_all(copies, REP, 0, 0, axis_index_groups=firsts, tiled=True)  9.33 us
    all_gather x1, blocking collectives, shards(): lax.all_gather(band, 'x', axis_index_groups=seconds)  6.45 us
    all_to_all x1, waiting for transfers between devices, shards(): lax.all_to_all(pieces, REP, 0, 0, axis_index_groups=[along_rep], tiled=True)  3.8 us
    pallas_call x1, Pallas kernels, shards(): pl.pallas_call(lambda *refs: finish_kernel(element_count, *refs), out_sha...  1.5 us
    all_to_all x1, waiting for transfers between devices, shards(): lax.all_to_all(shares.reshape(members, 1, LANES), NAMES, 0, 0, axis_index...  1.27 us
    sub x1, other arithmetic, shards(): base = master - 0.63 * kept  1.21 us
  transfers between devices with their start and end apart: 2, of which 2 were waited for; matrix products, arithmetic and copies ran while one was open for 2% of the time, Pallas kernels for 0%

profile of v8, /device:TPU:1, one launch (start us, length us, event | category | flops | bytes accessed | tf_op | source)
XLA Modules:
  0.0 56.6 jit_solution(10427402199213493437)
XLA Ops:
  0.6 0.0 copy-start
  0.6 9.9 %all-to-all-start = ((bf16[16,8,1280]{2,1,0:T(8,128)(2,1)}), bf16[16,8,1280]{2,1,0:T(8,128)(2,1)S(1)}, u32[]{:S(2)}, u32[]{:S(2)}) async-start(bf16[16,8,1280]{2,1,0:T(8,128)(2,1)} %bitcast.10), calls=%async_computation | async-start | bytes 655360 | tf_op jit(solution)/shard_map/all_to_all | solution.py:132
  10.6 0.0 copy-done
  10.6 0.0 dynamic-slice-start
  10.6 1.2 %multiply_subtract_fusion = (f32[16,10240]{1,0:T(8,128)S(1)}, f32[16,10240]{1,0:T(8,128)S(1)}) fusion(f32[16,10240]{1,0:T(8,128)S(1)} %copy-done, f32[16,10240]{1,0:T(8,128)} %param.5), kind=kLoop, calls=%fused_computation | loop fusion | flops 491520 | bytes 2621440 | tf_op jit(solution)/shard_map/sub | solution.py:137
  11.8 3.8 %all-to-all-done = bf16[16,8,1280]{2,1,0:T(8,128)(2,1)S(1)} async-done(((bf16[16,8,1280]{2,1,0:T(8,128)(2,1)}), bf16[16,8,1280]{2,1,0:T(8,128)(2,1)S(1)}, u32[]{:S(2)}, u32[]{:S(2)}) %all-to-all-start) | async-done | bytes 327712 | tf_op jit(solution)/shard_map/all_to_all | solution.py:132
  15.6 0.0 dynamic-slice-done
  15.6 0.1 subtract_reduce_fusion
  16.0 9.3 %all_to_all.15 = f16[8,8,1408]{2,1,0:T(8,128)(2,1)S(1)} all-to-all(f16[8,8,1408]{2,1,0:T(8,128)(2,1)S(1)} %broadcast_in_dim.5), channel_id=1, replica_groups={{448,480,384,416,64,96,0,32},{192,224,128,160,320,352,256,288},{449,481..., dimensions={0} | all-to-all | bytes 360448 | tf_op jit(solution)/shard_map/all_to_all | solution.py:143
  25.3 0.7 %shard_map.58 = f32[64,128]{1,0:T(8,128)} custom-call(f32[8,8,1408]{2,1,0:T(8,128)S(1)} %convert_element_type.17.coded_ref), custom_call_target="tpu_custom_call" | custom-call | flops 270336 | bytes 360448 | tf_op jit(solution)/shard_map/pallas_call | solution.py:148
  26.0 21.2 %all-to-all-start.2 = ((f32[64,1,128]{2,1,0:T(1,128)}), f32[64,1,128]{2,1,0:T(1,128)S(1)}, u32[]{:S(2)}, u32[]{:S(2)}) async-start(f32[64,1,128]{2,1,0:T(1,128)} %bitcast.4), calls=%async_computation.2 | async-start | bytes 65536 | tf_op jit(solution)/shard_map/all_to_all | solution.py:156
  47.3 6.5 %all-gather = f16[16,8,1408]{2,1,0:T(8,128)(2,1)S(1)} all-gather(f16[8,8,1408]{2,1,0:T(8,128)(2,1)S(1)} %all_to_all.15), channel_id=2, replica_groups={{384,256},{0,128},{385,257},{1,129},{386,258},{2,130},{387,259},{3,131}..., dimensions={0}, use_global_device_ids=true | all-gather | bytes 540672 | tf_op jit(solution)/shard_map/all_gather | solution.py:157
  53.8 1.3 %all-to-all-done.2 = f32[64,1,128]{2,1,0:T(1,128)S(1)} async-done(((f32[64,1,128]{2,1,0:T(1,128)}), f32[64,1,128]{2,1,0:T(1,128)S(1)}, u32[]{:S(2)}, u32[]{:S(2)}) %all-to-all-start.2) | async-done | bytes 32800 | tf_op jit(solution)/shard_map/all_to_all | solution.py:156
  55.1 1.5 %shard_map.59 = (f32[16,10240]{1,0:T(8,128)}, f32[16,10240]{1,0:T(8,128)}, bf16[16,10240]{1,0:T(8,128)(2,1)}) custom-call(f32[64,128]{1,0:T(8,128)S(1)} %bitcast.9, f32[16,8,1408]{2,1,0:T(8,128)S(1)} %convert_element_type.21.refs_1_, f32[16,10240]{1,0:T(8,128)S(1)} %get-tuple-element.7.refs_2_, f32[16,10240]{1,0:T(8,128)S(1)} %get-tuple-element.8.refs_3_), custom_call_target="tpu_custom_call" | custom-call | flops 1310720 | bytes 3604480 | tf_op jit(solution)/shard_map/pallas_call | solution.py:161
  (15 shorter events, 0.3 us)
Async XLA Ops:
  0.6 9.9 %copy-start = (f32[16,10240]{1,0:T(8,128)S(1)}, f32[16,10240]{1,0:T(8,128)}, u32[]{:S(2)}) copy-start(f32[16,10240]{1,0:T(8,128)} %param.4) | copy-start | bytes 1966084
  0.6 15.0 %all-to-all-start = ((bf16[16,8,1280]{2,1,0:T(8,128)(2,1)}), bf16[16,8,1280]{2,1,0:T(8,128)(2,1)S(1)}, u32[]{:S(2)}, u32[]{:S(2)}) async-start(bf16[16,8,1280]{2,1,0:T(8,128)(2,1)} %bitcast.10), calls=%async_computation | async-start | bytes 655360 | tf_op jit(solution)/shard_map/all_to_all | solution.py:132
  10.6 5.0 %dynamic-slice-start = ((f32[16,10240]{1,0:T(8,128)}, s32[]{:T(128)}, s32[]{:T(128)}), f32[8,1280]{1,0:T(8,128)S(1)}, s32[]{:S(2)}) async-start(f32[16,10240]{1,0:T(8,128)} %param.4, s32[]{:T(128)} %select_n.28, s32[]{:T(128)} %select_n.30), calls=%async_computation.3 | async-start | bytes 82432 | tf_op jit(solution)/shard_map/dynamic_slice | solution.py:134
  26.0 29.0 %all-to-all-start.2 = ((f32[64,1,128]{2,1,0:T(1,128)}), f32[64,1,128]{2,1,0:T(1,128)S(1)}, u32[]{:S(2)}, u32[]{:S(2)}) async-start(f32[64,1,128]{2,1,0:T(1,128)} %bitcast.4), calls=%async_computation.2 | async-start | bytes 65536 | tf_op jit(solution)/shard_map/all_to_all | solution.py:156
